TPU v7x, 256 devices: a whole 4x4x8 slice. The times are simulated.
256 devices in a mesh: row: 16 (over z, x_hi), col: 16 (over y, x_lo, core).
Axes of the slice: x: 4 (x_hi: 2, x_lo: 2; x = x_hi * 2 + x_lo), y: 4, z: 8, core: 2. Of those that a mesh axis runs over, the one named last changes fastest.
Arguments:
- affinity_tiles: bfloat16 [16, 16, 80, 128, 128], P('row', 'col'), may hold values from -14983200 to 14983200, as said below
- tile_index: int32 [16, 16, 2, 80], P('row', 'col'), may hold values from 0 to 15, as said below
- start_block: bfloat16 [32768, 128], P(('row', 'col')), may hold values from -6 to 6
Outputs:
- ritz_block: float32 [32768, 128], P(('row', 'col'))
- ritz_gram: float32 [128, 128], replicated
Inputs may be any that keep to these rules, and one draw needn't show every extreme that they name: `tile_index`: each device's slots name distinct tiles of its block; the tile pattern of A is symmetric and holds every diagonal tile; slots without a tile carry indices 0 and 0 and a zero tile. `affinity_tiles`: A is symmetric: the tile at tile row I and tile column J is the transpose of the tile at J and I; every diagonal entry of A is 1 or more.
All inputs are finite; a program needn't handle non-finite values.
Results may differ from a plain program's by a relative error of at most 0.00115.
The roundings to bfloat16 on the way count: a program that leaves them out, or rounds other values in their place, can miss the bound.
Values may be sent and summed in bfloat16 or wider, within the bound.
A program may use at most 64 MiB of HBM per device.

v0:
```python
import jax
import jax.numpy as jnp
from jax import lax
from jax.sharding import PartitionSpec as P

POWER = 3


def local(affinity_tiles, tile_index, start_block):
    stored = affinity_tiles[0, 0]
    index = tile_index[0, 0]
    rows_axis = lax.axis_size("row")
    cols_axis = lax.axis_size("col")
    edge = stored.shape[-1]
    width = start_block.shape[1]
    per_device = start_block.shape[0] // edge
    order = edge * per_device * rows_axis * cols_axis
    row_local = jax.ops.segment_max(
        jnp.max(jnp.abs(stored), axis=2).astype(jnp.float32),
        index[0],
        num_segments=per_device * cols_axis,
    )
    col_local = jax.ops.segment_max(
        jnp.max(jnp.abs(stored), axis=1).astype(jnp.float32),
        index[1],
        num_segments=per_device * rows_axis,
    )
    row_peak = lax.pmax(jnp.maximum(row_local, 0.0).reshape(-1), "col")
    col_peak = lax.pmax(jnp.maximum(col_local, 0.0).reshape(-1), "row")
    row_scale = 1.0 / jnp.sqrt(row_peak)
    col_scale = 1.0 / jnp.sqrt(col_peak)
    mine_rows = lax.dynamic_slice_in_dim(
        row_scale, lax.axis_index("col") * (per_device * edge), per_device * edge
    )[:, None]
    mine_cols = lax.dynamic_slice_in_dim(
        col_scale, lax.axis_index("row") * (per_device * edge), per_device * edge
    )[:, None]

    def along(gathered):
        blocks = gathered.reshape(-1, edge, width)
        picked = blocks[index[1]]
        terms = jnp.einsum("sab,sbv->sav", stored, picked, preferred_element_type=jnp.float32)
        summed = jax.ops.segment_sum(terms, index[0], num_segments=per_device * cols_axis)
        return lax.psum_scatter(summed.reshape(-1, width), "col", scatter_dimension=0, tiled=True)

    weighted = (mine_rows * start_block.astype(jnp.float32)).astype(jnp.bfloat16)
    power = None
    for step in range(POWER):
        if step % 2 == 0:
            across_gathered = lax.all_gather(weighted, "col", axis=0, tiled=True).reshape(
                -1, edge, width
            )
            across_picked = across_gathered[index[0]]
            across_terms = jnp.einsum(
                "sab,sav->sbv", stored, across_picked, preferred_element_type=jnp.float32
            )
            across_summed = jax.ops.segment_sum(
                across_terms, index[1], num_segments=per_device * rows_axis
            )
            power = lax.psum_scatter(
                across_summed.reshape(-1, width), "row", scatter_dimension=0, tiled=True
            )
            owned = mine_cols
        else:
            power = along(lax.all_gather(weighted, "row", axis=0, tiled=True))
            owned = mine_rows
        if step + 1 < POWER:
            weighted = (owned * owned * power).astype(jnp.bfloat16)
    iterate = mine_cols * power
    local_gram = jnp.dot(
        iterate.T, iterate, precision=lax.Precision.HIGHEST, preferred_element_type=jnp.float32
    )
    gram = lax.psum(local_gram, ("row", "col")) / order
    lower = jnp.linalg.cholesky(gram)
    basis = jax.scipy.linalg.solve_triangular(lower, iterate.T, lower=True).T
    scaled_basis = (mine_cols * basis).astype(jnp.bfloat16)
    gathered = lax.all_gather(scaled_basis, "row", axis=0, tiled=True)
    ritz_block = mine_rows * along(gathered)
    local_ritz = jnp.dot(
        ritz_block.T,
        ritz_block,
        precision=lax.Precision.HIGHEST,
        preferred_element_type=jnp.float32,
    )
    ritz_gram = lax.psum(local_ritz, ("row", "col")) / order
    return (ritz_block, ritz_gram)


def solution(mesh):
    placed = (
        P("row", "col", None, None, None),
        P("row", "col", None, None),
        P(("row", "col"), None),
    )
    return jax.shard_map(
        local, mesh=mesh, in_specs=placed, out_specs=(P(("row", "col"), None), P()), check_vma=False
    )
```

profile of v0, /device:TPU:1, one launch (start us, length us, event | category | flops | bytes accessed | tf_op | source)
XLA Modules:
  0.0 1336.3 jit_solution(11991331873623068466)
XLA Ops:
  7.2 0.8 slice_bitcast_fusion
  8.0 0.8 fusion.38
  8.7 2.8 fusion.20
  11.6 1.0 scatter_custom_fusion
  12.6 30.1 %pmax.14 = f32[2048]{0:T(1024)S(1)} all-reduce(f32[2048]{0:T(1024)S(1)} %maximum_bitcast_fusion.1), channel_id=1, replica_groups=mesh['row'=16,'col'=16] {'col'}, use_global_device_ids=true, to_apply=%region_2.0 | all-reduce | flops 2048 | bytes 16384 | tf_op jit(solution)/shard_map/pmax | solution.py:28
  42.9 21.0 %all_gather.12 = bf16[2048,128]{1,0:T(8,128)(2,1)S(1)} all-gather(bf16[128,128]{1,0:T(8,128)(2,1)S(1)} %multiply_convert_fusion.2), channel_id=1, replica_groups=mesh['row'=16,'col'=16] {'col'}, dimensions={0}, use_global_device_ids=true | all-gather | bytes 557056 | tf_op jit(solution)/shard_map/all_gather | solution.py:50
  64.0 2.5 gather_fusion
  66.5 5.1 fusion.8
  71.6 5.9 copy.14
  77.5 1.1 broadcast.108.clone.2
  78.7 17.3 %scatter_fusion = f32[16,128,128]{2,1,0:T(8,128)} fusion(f32[16,128,128]{2,1,0:T(8,128)} %broadcast.108.clone.2, s32[80]{0:T(128)S(1)} %get-tuple-element.14, f32[80,128,128]{2,1,0:T(8,128)} %copy.14), kind=kCustom, calls=%fused_computation.6 | custom fusion | flops 1310720 | bytes 15728960 | tf_op jit(solution)/shard_map/scatter-add | solution.py:57
  96.1 0.9 scatter_custom_fusion.1
  97.0 38.1 %pmax.15 = f32[2048]{0:T(1024)S(1)} all-reduce(f32[2048]{0:T(1024)S(1)} %maximum_bitcast_fusion), channel_id=1, replica_groups=mesh['row'=16,'col'=16] {'row'}, use_global_device_ids=true, to_apply=%region_5.0 | all-reduce | flops 2048 | bytes 16384 | tf_op jit(solution)/shard_map/pmax | solution.py:29
  135.2 158.5 %reduce-scatter.5.cloned.1.call-done = f32[128,128]{1,0:T(8,128)} async-done(((f32[2048,128]{1,0:T(8,128)}), f32[128,128]{1,0:T(8,128)}) %reduce-scatter.5.cloned.1.call-update) | async-done | bytes 65552 | tf_op jit(solution)/shard_map/reduce_scatter | solution.py:60
  293.7 0.9 multiply_convert_fusion.1
  294.6 33.8 %all_gather.13 = bf16[2048,128]{1,0:T(8,128)(2,1)S(1)} all-gather(bf16[128,128]{1,0:T(8,128)(2,1)S(1)} %multiply_convert_fusion.1), channel_id=1, replica_groups=mesh['row'=16,'col'=16] {'row'}, dimensions={0}, use_global_device_ids=true | all-gather | bytes 557056 | tf_op jit(solution)/shard_map/all_gather | solution.py:65
  328.4 2.5 gather_fusion.1
  331.0 6.1 fusion.11
  337.0 5.9 copy.16
  342.9 1.1 broadcast.108.clone.1
  344.1 16.6 %scatter_fusion.1 = f32[16,128,128]{2,1,0:T(8,128)} fusion(f32[16,128,128]{2,1,0:T(8,128)} %broadcast.108.clone.1, s32[80]{0:T(128)S(1)} %get-tuple-element.15, f32[80,128,128]{2,1,0:T(8,128)} %copy.16), kind=kCustom, calls=%fused_computation.7 | custom fusion | flops 1310720 | bytes 15728960 | tf_op jit(solution)/shard_map/scatter-add | solution.py:43
  360.7 71.1 %reduce-scatter.7.cloned.1.call-done = f32[128,128]{1,0:T(8,128)} async-done(((f32[2048,128]{1,0:T(8,128)}), f32[128,128]{1,0:T(8,128)}) %reduce-scatter.7.cloned.1.call-update) | async-done | bytes 65552 | tf_op jit(solution)/shard_map/reduce_scatter | solution.py:44
  431.8 0.9 multiply_convert_fusion
  432.7 22.9 %all_gather.14 = bf16[2048,128]{1,0:T(8,128)(2,1)S(1)} all-gather(bf16[128,128]{1,0:T(8,128)(2,1)S(1)} %multiply_convert_fusion), channel_id=1, replica_groups=mesh['row'=16,'col'=16] {'col'}, dimensions={0}, use_global_device_ids=true | all-gather | bytes 557056 | tf_op jit(solution)/shard_map/all_gather | solution.py:50
  455.6 2.5 gather_fusion.2
  458.2 5.1 fusion.14
  463.3 5.9 copy.18
  469.2 1.1 broadcast.108.clone
  470.3 17.3 %scatter_fusion.2 = f32[16,128,128]{2,1,0:T(8,128)} fusion(f32[16,128,128]{2,1,0:T(8,128)} %broadcast.108.clone, s32[80]{0:T(128)S(1)} %get-tuple-element.14, f32[80,128,128]{2,1,0:T(8,128)} %copy.18), kind=kCustom, calls=%fused_computation.8 | custom fusion | flops 1310720 | bytes 15728960 | tf_op jit(solution)/shard_map/scatter-add | solution.py:57
  487.7 196.3 %reduce-scatter.9.cloned.1.call-done = f32[128,128]{1,0:T(8,128)} async-done(((f32[2048,128]{1,0:T(8,128)}), f32[128,128]{1,0:T(8,128)}) %reduce-scatter.9.cloned.1.call-update) | async-done | bytes 65552 | tf_op jit(solution)/shard_map/reduce_scatter | solution.py:60
  684.0 1.9 fusion.27
  685.9 246.2 %all-reduce.3.cloned.1.call-done = f32[128,128]{0,1:T(8,128)} async-done(((f32[128,128]{0,1:T(8,128)}), f32[128,128]{0,1:T(8,128)}) %all-reduce.3.cloned.1.call-update) | async-done | bytes 65552 | tf_op jit(solution)/shard_map/psum | solution.py:73
  932.2 0.8 broadcast_multiply_fusion.1
  933.1 0.9 fusion.25
  934.0 11.7 cholesky.16
  947.0 9.8 custom-call.7
  956.9 1.1 fusion.22
  958.0 33.8 %all_gather.15 = bf16[2048,128]{1,0:T(8,128)(2,1)S(1)} all-gather(bf16[128,128]{1,0:T(8,128)(2,1)S(1)} %fusion.22), channel_id=1, replica_groups=mesh['row'=16,'col'=16] {'row'}, dimensions={0}, use_global_device_ids=true | all-gather | bytes 557056 | tf_op jit(solution)/shard_map/all_gather | solution.py:77
  991.8 2.5 gather_fusion.3
  994.3 6.0 fusion.17
  1000.4 6.0 copy.22
  1006.4 10.8 scatter_fusion.3
  1017.3 1.0 copy-done.1
  1018.3 63.9 %reduce-scatter.11.cloned.1.call-done = f32[128,128]{1,0:T(8,128)} async-done(((f32[2048,128]{1,0:T(8,128)}), f32[128,128]{1,0:T(8,128)}) %reduce-scatter.11.cloned.1.call-update) | async-done | bytes 65552 | tf_op jit(solution)/shard_map/reduce_scatter | solution.py:44
  1082.2 0.9 broadcast_multiply_fusion.2
  1083.2 0.9 fusion.41
  1084.1 243.8 %all-reduce.5.cloned.1.call-done = f32[128,128]{0,1:T(8,128)} async-done(((f32[128,128]{0,1:T(8,128)}), f32[128,128]{0,1:T(8,128)}) %all-reduce.5.cloned.1.call-update) | async-done | bytes 65552 | tf_op jit(solution)/shard_map/psum | solution.py:85
  1327.9 0.8 broadcast_multiply_fusion
  (32 shorter events, 2.9 us)
Async XLA Ops:
  7.2 35.7 %copy-start.3 = (bf16[128,128]{1,0:T(8,128)(2,1)S(1)}, bf16[128,128]{1,0:T(8,128)(2,1)}, u32[]{:S(2)}) copy-start(bf16[128,128]{1,0:T(8,128)(2,1)} %param.5) | copy-start | bytes 98308
  7.2 286.5 %reduce-scatter.5.cloned.1.call-start = ((), (), s32[]{:S(2)}) async-start(), calls=%async_computation.4 | async-start | bytes 1114112 | tf_op jit(solution)/shard_map/reduce_scatter | solution.py:60
  63.9 2.5 copy-start
  96.0 335.8 %reduce-scatter.7.cloned.1.call-start = ((), (), s32[]{:S(2)}) async-start(), calls=%async_computation.5 | async-start | bytes 1114112 | tf_op jit(solution)/shard_map/reduce_scatter | solution.py:44
  360.6 323.3 %reduce-scatter.9.cloned.1.call-start = ((), (), s32[]{:S(2)}) async-start(), calls=%async_computation.6 | async-start | bytes 1114112 | tf_op jit(solution)/shard_map/reduce_scatter | solution.py:60
  487.7 444.5 %all-reduce.3.cloned.1.call-start = ((), (), s32[]{:S(2)}) async-start(), calls=%async_computation.7 | async-start | bytes 131072 | tf_op jit(solution)/shard_map/psum | solution.py:73
  685.9 396.4 %reduce-scatter.11.cloned.1.call-start = ((), (), s32[]{:S(2)}) async-start(), calls=%async_computation.8 | async-start | bytes 1114112 | tf_op jit(solution)/shard_map/reduce_scatter | solution.py:44
  1017.3 1.0 copy-start.1
  1018.3 309.6 %all-reduce.5.cloned.1.call-start = ((), (), s32[]{:S(2)}) async-start(), calls=%async_computation.9 | async-start | bytes 131072 | tf_op jit(solution)/shard_map/psum | solution.py:85
  1083.2 246.3 %copy-start.2 = (f32[128,128]{1,0:T(8,128)}, f32[128,128]{1,0:T(8,128)S(1)}, u32[]{:S(2)}) copy-start(f32[128,128]{1,0:T(8,128)S(1)} %broadcast_multiply_fusion.2) | copy-start | bytes 196612
Sparse Core Ops, SparseCore 0:
  96.1 197.5 reduce-scatter.4
  360.8 70.9 reduce-scatter.6
  487.8 196.1 reduce-scatter.8
  690.8 241.3 all-reduce.2
  1018.4 63.8 reduce-scatter.10
  1088.2 239.6 all-reduce.4
where the time goes:
time: 1340 us
  waiting for transfers between devices  980 us (73%)
  blocking collectives  180 us (13%)
  other arithmetic  95.9 us (7%)
  local copies, waits for them, and re-layouts  39.9 us (3%)
  matrix products  26.2 us (2%)
  between operations  14.3 us (1%)
    reduce_scatter x2, waiting for transfers between devices, local(): lax.psum_scatter(across_summed.reshape(-1, width), 'row', scatter_dimensi...  355 us
    psum x1, waiting for transfers between devices, local(): gram = lax.psum(local_gram, ('row', 'col')) / order  246 us
    psum x1, waiting for transfers between devices, local(): ritz_gram = lax.psum(local_ritz, ('row', 'col')) / order  244 us
    reduce_scatter x2, waiting for transfers between devices, along(): lax.psum_scatter(summed.reshape(-1, width), 'col', scatter_dimension=0, t...  135 us
    all_gather x2, blocking collectives, local(): lax.all_gather(weighted, 'col', axis=0, tiled=True).reshape(-1, edge, width)  43.9 us
    pmax x1, blocking collectives, local(): col_peak = lax.pmax(jnp.maximum(col_local, 0.0).reshape(-1), 'row')  38.1 us
    scatter-add x2, other arithmetic, local(): jax.ops.segment_sum(across_terms, index[1], num_segments=per_device * row...  34.6 us
    all_gather x1, blocking collectives, local(): gathered = lax.all_gather(scaled_basis, 'row', axis=0, tiled=True)  33.8 us
  transfers between devices with their start and end apart: 6, of which 6 were waited for; matrix products, arithmetic and copies ran while one was open for 0% of the time, Pallas kernels for 0%

commit v1 on v0

v1 whole, which is shorter than its diff:
```python
import functools

import jax
import jax.numpy as jnp
from jax import lax
from jax.experimental import pallas as pl
from jax.experimental.pallas import tpu as pltpu
from jax.sharding import PartitionSpec as P

EDGE = 128
PANEL = 16
MESH = pl.DeviceIdType.MESH
HIGH = lax.Precision.HIGHEST
F32 = jnp.float32
BF16 = jnp.bfloat16


def kernel(
    nr, nc, slots, order,
    tiles_hbm, table, cell, start_ref,
    ritz_ref, gram_ref,
    tiles, dense, rbuf, cbuf, scale_r, scale_c,
    own_s, own_w, sT, w1, w2, w3, w4,
    parts, lands, gpart, ga, gs, gb, gfull, elim,
    load_sem, send_sem, recv_sem,
):
    me_r = lax.axis_index("row")
    me_c = lax.axis_index("col")
    size = {"row": nr, "col": nc}
    me_of = {"row": me_r, "col": me_c}

    def lanes(tile):
        return pl.ds(pl.multiple_of(tile * EDGE, EDGE), EDGE)

    def copy(x, axis, peer, src, dst):
        return pltpu.make_async_remote_copy(
            src_ref=src, dst_ref=dst,
            send_sem=send_sem.at[x, peer], recv_sem=recv_sem.at[x, me_of[axis]],
            device_id={axis: peer}, device_id_type=MESH,
        )

    def send_all(x, axis, src_of, dst):
        n, me = size[axis], me_of[axis]

        @pl.loop(1, n)
        def _(k):
            peer = lax.rem(me + k, n)
            copy(x, axis, peer, src_of(peer), dst).start()

    def wait_from(x, axis, source, ref):
        pltpu.make_async_remote_copy(
            src_ref=ref, dst_ref=ref,
            send_sem=send_sem.at[x, source], recv_sem=recv_sem.at[x, source],
            device_id={axis: source}, device_id_type=MESH,
        ).wait_recv()

    def wait_all(x, axis, dst_of):
        n, me = size[axis], me_of[axis]

        @pl.loop(1, n)
        def _(k):
            source = lax.rem(me + k, n)
            wait_from(x, axis, source, dst_of(source))

    def drain(x, axis, ref):
        n, me = size[axis], me_of[axis]

        @pl.loop(1, n)
        def _(k):
            peer = lax.rem(me + k, n)
            copy(x, axis, peer, ref, ref).wait_send()

    load = pltpu.make_async_copy(tiles_hbm, tiles.at[pl.ds(0, slots)], load_sem)
    load.start()
    barrier = pltpu.get_barrier_semaphore()
    for axis in ("row", "col"):
        @pl.loop(1, size[axis])
        def _(k):
            peer = lax.rem(me_of[axis] + k, size[axis])
            pl.semaphore_signal(barrier, inc=1, device_id={axis: peer}, device_id_type=MESH)
    own_s[...] = start_ref[...].astype(F32).T.astype(BF16)
    sT[:, lanes(me_c)] = own_s[...]
    tiles[slots] = jnp.zeros((EDGE, EDGE), BF16)
    pl.semaphore_wait(barrier, nr + nc - 2)

    send_all(0, "col", lambda peer: own_s, sT.at[:, lanes(me_c)])

    load.wait()

    def fold(s, total):
        return total + jnp.where(cell[s] == 0, tiles[s], jnp.zeros((EDGE, EDGE), BF16))

    corner = lax.fori_loop(0, slots, fold, jnp.zeros((EDGE, EDGE), BF16))

    @pl.loop(0, nc)
    def _(i):
        most = jnp.zeros((EDGE, EDGE), BF16)
        for j in range(nr):
            tile = tiles[table[i * nr + j]]
            if j == 0:
                tile = jnp.where(i == 0, corner, tile)
            dense[lanes(i), j * EDGE:(j + 1) * EDGE] = tile
            most = jnp.maximum(most, jnp.abs(tile))
        rbuf[me_c, pl.ds(i, 1), :] = jnp.max(most.astype(F32).T, axis=0, keepdims=True)

    send_all(1, "col", lambda peer: rbuf.at[me_c], rbuf.at[me_c])

    @pl.loop(0, nr)
    def _(j):
        most = jnp.zeros((EDGE, EDGE), BF16)
        for i in range(nc):
            most = jnp.maximum(most, jnp.abs(dense[i * EDGE:(i + 1) * EDGE, lanes(j)]))
        cbuf[me_r, pl.ds(j, 1), :] = jnp.max(most.astype(F32), axis=0, keepdims=True)

    send_all(2, "row", lambda peer: cbuf.at[me_r], cbuf.at[me_r])
    wait_all(1, "col", lambda source: rbuf.at[source])
    scale_r[...] = 1.0 / jnp.sqrt(jnp.max(rbuf[...], axis=0))
    wait_all(0, "col", lambda source: sT.at[:, lanes(source)])

    for t in range(nc):
        here = slice(t * EDGE, (t + 1) * EDGE)
        w1[:, here] = (scale_r[t:t + 1, :] * sT[:, here].astype(F32)).astype(BF16)

    def product(x, which, axis, w):
        n, me = size[axis], me_of[axis]
        half = n // 2
        part, land = parts.at[which], lands.at[which]

        @pl.loop(0, half)
        def _(q):
            pair = lax.rem(me // 2 + 1 + q, half)
            wide = pl.ds(pl.multiple_of(pair * 2 * EDGE, 2 * EDGE), 2 * EDGE)
            if axis == "row":
                y = jnp.dot(w[...], dense[:, wide], preferred_element_type=F32)
            else:
                y = lax.dot_general(
                    w[...], dense[wide, :], (((1,), (1,)), ((), ())), preferred_element_type=F32
                )
            for h in range(2):
                peer = pair * 2 + h
                part[peer] = y[:, h * EDGE:(h + 1) * EDGE]

                @pl.when(peer != me)
                def _():
                    copy(x, axis, peer, part.at[peer], land.at[me]).start()

        def add(k, total):
            source = lax.rem(me + k, n)
            wait_from(x, axis, source, land.at[source])
            return total + land[source]

        return lax.fori_loop(1, n, add, part[me])

    def spread(x, axis, tile, w):
        slot = 0 if w is w2 else (1 if w is w3 else 2)
        me = me_of[axis]
        own_w[slot] = tile
        send_all(x, axis, lambda peer: own_w.at[slot], w.at[:, lanes(me)])
        w[:, lanes(me)] = tile
        wait_all(x, axis, lambda source: w.at[:, lanes(source)])

    share = EDGE // nc

    def eighth(p):
        return pl.ds(pl.multiple_of(p * share, share), share)

    def gram_sum(x, which, local):
        part, a, s, b, full = gpart.at[which], ga.at[which], gs.at[which], gb.at[which], gfull.at[which]
        part[...] = local
        send_all(x, "col", lambda peer: part.at[eighth(peer)], a.at[me_c])
        a[me_c] = part[eighth(me_c), :]
        wait_all(x, "col", lambda source: a.at[source])
        mine = jnp.sum(a[...], axis=0)
        s[...] = mine
        send_all(x + 1, "row", lambda peer: s, b.at[me_r])
        b[me_r] = mine
        wait_all(x + 1, "row", lambda source: b.at[source])
        full[eighth(me_c), :] = jnp.sum(b[...], axis=0) / order
        send_all(x + 2, "col", lambda peer: full.at[eighth(me_c)], full.at[eighth(me_c)])
        wait_all(x + 2, "col", lambda source: full.at[eighth(source)])
        return full[...]

    def gram_drain(x, which):
        drain(x, "col", gpart.at[which, pl.ds(0, share)])
        drain(x + 1, "row", gs.at[which])
        drain(x + 2, "col", gpart.at[which, pl.ds(0, share)])

    p1 = product(3, 0, "row", w1)
    wait_all(2, "row", lambda source: cbuf.at[source])
    scale_c[...] = 1.0 / jnp.sqrt(jnp.max(cbuf[...], axis=0))
    mine_c = scale_c[pl.ds(me_r, 1), :]
    mine_r = scale_r[pl.ds(me_c, 1), :]
    spread(4, "row", (mine_c * mine_c * p1).astype(BF16), w2)
    p2 = product(5, 1, "col", w2)
    spread(6, "col", (mine_r * mine_r * p2).astype(BF16), w3)
    p3 = product(7, 2, "row", w3)
    iterate = mine_c * p3

    def outer(v):
        return lax.dot_general(
            v, v, (((1,), (1,)), ((), ())), precision=HIGH, preferred_element_type=F32
        )

    gram = gram_sum(8, 0, outer(iterate))

    elim[:, :EDGE] = gram
    row_id = lax.broadcasted_iota(jnp.int32, (EDGE, EDGE), 0)
    lane_id = lax.broadcasted_iota(jnp.int32, (EDGE, EDGE), 1)
    elim[:, EDGE:] = jnp.where(row_id == lane_id, 1.0, 0.0)
    lane = lax.broadcasted_iota(jnp.int32, (PANEL, EDGE), 1)
    sub = lax.broadcasted_iota(jnp.int32, (PANEL, EDGE), 0)

    @pl.loop(0, EDGE // PANEL)
    def _(p):
        rows = pl.ds(pl.multiple_of(p * PANEL, PANEL), PANEL)
        left = elim[rows, :EDGE]
        right = elim[rows, EDGE:]
        column = [
            jnp.broadcast_to(
                jnp.sum(jnp.where(lane == p * PANEL + k, left, 0.0), axis=1, keepdims=True),
                (PANEL, EDGE),
            )
            for k in range(PANEL)
        ]
        for k in range(PANEL):
            inv = 1.0 / jnp.sqrt(column[k][k:k + 1, :])
            step = jnp.where(sub > k, column[k] * inv, 0.0)
            l_row = left[k:k + 1, :] * inv
            r_row = right[k:k + 1, :] * inv
            left = jnp.where(sub == k, l_row, left - step * l_row)
            right = jnp.where(sub == k, r_row, right - step * r_row)
            for m in range(k + 1, PANEL):
                column[m] = column[m] - step * (column[m][k:k + 1, :] * inv)
        elim[rows, :EDGE] = left
        elim[rows, EDGE:] = right
        later = jnp.where(lane >= (p + 1) * PANEL, left, 0.0)
        whole = jnp.concatenate([left, right], axis=1)
        elim[...] -= lax.dot_general(
            later, whole, (((0,), (0,)), ((), ())), precision=HIGH, preferred_element_type=F32
        )

    basis = jnp.dot(elim[:, EDGE:], iterate, precision=HIGH, preferred_element_type=F32)
    spread(11, "row", (mine_c * basis).astype(BF16), w4)
    p4 = product(12, 3, "col", w4)
    ritz = mine_r * p4
    ritz_ref[...] = ritz.T
    gram_ref[...] = gram_sum(13, 1, outer(ritz))

    drain(0, "col", own_s)
    drain(1, "col", rbuf.at[me_c])
    drain(2, "row", cbuf.at[me_r])
    drain(3, "row", parts.at[0, 0])
    drain(4, "row", own_s)
    drain(5, "col", parts.at[0, 0])
    drain(6, "col", own_s)
    drain(7, "row", parts.at[0, 0])
    gram_drain(8, 0)
    drain(11, "row", own_s)
    drain(12, "col", parts.at[0, 0])
    gram_drain(13, 1)


def local(affinity_tiles, tile_index, start_block):
    nr, nc = lax.axis_size("row"), lax.axis_size("col")
    stored = affinity_tiles[0, 0]
    index = tile_index[0, 0]
    slots = stored.shape[0]
    cell = index[0] * nr + index[1]
    hit = cell[:, None] == jnp.arange(nr * nc, dtype=jnp.int32)[None, :]
    number = jnp.arange(slots, dtype=jnp.int32)[:, None]
    table = jnp.min(jnp.where(hit, number, slots), axis=0)
    most = max(nr, nc)
    share = EDGE // nc
    tile = (EDGE, EDGE)
    vmem = pltpu.VMEM
    return pl.pallas_call(
        functools.partial(kernel, nr, nc, slots, nr * nc * EDGE),
        out_shape=(jax.ShapeDtypeStruct(tile, F32), jax.ShapeDtypeStruct(tile, F32)),
        in_specs=[
            pl.BlockSpec(memory_space=pl.ANY),
            pl.BlockSpec(memory_space=pltpu.SMEM),
            pl.BlockSpec(memory_space=pltpu.SMEM),
            pl.BlockSpec(memory_space=pltpu.VMEM),
        ],
        out_specs=(pl.BlockSpec(memory_space=pltpu.VMEM), pl.BlockSpec(memory_space=pltpu.VMEM)),
        scratch_shapes=[
            vmem((slots + 1, *tile), BF16),
            vmem((nc * EDGE, nr * EDGE), BF16),
            vmem((nc, nc, EDGE), F32),
            vmem((nr, nr, EDGE), F32),
            vmem((nc, EDGE), F32),
            vmem((nr, EDGE), F32),
            vmem(tile, BF16),
            vmem((3, *tile), BF16),
            vmem((EDGE, nc * EDGE), BF16),
            vmem((EDGE, nc * EDGE), BF16),
            vmem((EDGE, nr * EDGE), BF16),
            vmem((EDGE, nc * EDGE), BF16),
            vmem((EDGE, nr * EDGE), BF16),
            vmem((4, most, *tile), F32),
            vmem((4, most, *tile), F32),
            vmem((2, *tile), F32),
            vmem((2, nc, share, EDGE), F32),
            vmem((2, share, EDGE), F32),
            vmem((2, nr, share, EDGE), F32),
            vmem((2, *tile), F32),
            vmem((EDGE, 2 * EDGE), F32),
            pltpu.SemaphoreType.DMA,
            pltpu.SemaphoreType.DMA((16, most)),
            pltpu.SemaphoreType.DMA((16, most)),
        ],
        compiler_params=pltpu.CompilerParams(
            collective_id=0, has_side_effects=True, vmem_limit_bytes=48 * 2**20
        ),
    )(stored, table, cell, start_block)


def solution(mesh):
    placed = (
        P("row", "col", None, None, None),
        P("row", "col", None, None),
        P(("row", "col"), None),
    )
    return jax.shard_map(
        local, mesh=mesh, in_specs=placed, out_specs=(P(("row", "col"), None), P()), check_vma=False
    )
```

time: 1340 us -> 194 us (0.14)
  waiting for transfers between devices: 980 us -> 0 us
  Pallas kernels: 0 us -> 188 us
  blocking collectives: 180 us -> 0 us
  other arithmetic: 95.9 us -> 0.85 us
  local copies, waits for them, and re-layouts: 39.9 us -> 3.75 us
  matrix products: 26.2 us -> 0 us
  between operations: 14.3 us -> 0.65 us
    psum x2 -> x0, waiting for transfers between devices: 490 us -> none  [the longest x1 246 us: local(): gram = lax.psum(local_gram, ('row', 'col')) / order]
    reduce_scatter x4 -> x0, waiting for transfers between devices: 490 us -> none  [the longest x2 355 us: local(): lax.psum_scatter(across_summed.reshape(-1, width), 'row', scatter_dimensi...]
    pallas_call x0 -> x1, Pallas kernels: none -> 188 us  [local(): pl.pallas_call(functools.partial(kernel, nr, nc, slots, nr * nc * EDGE),...]
    all_gather x4 -> x0, blocking collectives: 112 us -> none  [the longest x2 43.9 us: local(): lax.all_gather(weighted, 'col', axis=0, tiled=True).reshape(-1, edge, width)]
    pmax x2 -> x0, blocking collectives: 68.2 us -> none  [the longest x1 38.1 us: local(): col_peak = lax.pmax(jnp.maximum(col_local, 0.0).reshape(-1), 'row')]
    scatter-add x4 -> x0, other arithmetic: 62 us -> none  [the longest x2 34.6 us: local(): jax.ops.segment_sum(across_terms, index[1], num_segments=per_device * row...]
    dot_general x6 -> x0, matrix products: 25.1 us -> none  [the longest x2 12.1 us: along(): jnp.einsum('sab,sbv->sav', stored, picked, preferred_element_type=jnp.flo...]
    another operation x7 -> x0, other arithmetic: 24.8 us -> none  [the longest x3 12.4 us: local(): lower = jnp.linalg.cholesky(gram)]
  transfers between devices with their start and end apart: 6 -> 0, of which waited for: 6 -> 0; matrix products, arithmetic and copies ran while one was open for 0% -> 0% of each run, Pallas kernels for 0% -> 0%
where the time goes in v1:
time: 194 us
  Pallas kernels  188 us (97%)
  local copies, waits for them, and re-layouts  3.75 us (2%)
    pallas_call x1, Pallas kernels, local(): pl.pallas_call(functools.partial(kernel, nr, nc, slots, nr * nc * EDGE),...  188 us

profile of v1, /device:TPU:1, one launch (start us, length us, event | category | flops | bytes accessed | tf_op | source)
XLA Modules:
  0.0 193.6 jit_solution(13866163651419795198)
XLA Ops:
  0.6 0.8 add_bitcast_fusion.cell
  1.4 0.1 select_reduce_fusion.table
  1.5 0.0 copy-start
  1.5 1.7 copy-done
  3.2 0.0 copy-start.1
  3.2 0.8 copy-done.1
  4.0 188.3 %shard_map.50 = (f32[128,128]{1,0:T(8,128)S(1)}, f32[128,128]{1,0:T(8,128)S(1)}) custom-call(bf16[80,128,128]{2,1,0:T(8,128)(2,1)S(1)} %bitcast.3, s32[256]{0:T(256)S(1)} %select_reduce_fusion.table, s32[80]{0:T(128)S(1)} %add_bitcast_fusion.cell, bf16[128,128]{1,0:T(8,128)(2,1)S(1)} %copy-done.1), custom_call_target="tpu_custom_call" | custom-call | tf_op jit(solution)/shard_map/pallas_call | solution.py:276
  192.3 0.6 copy.7
  193.0 0.6 copy.8
Async XLA Ops:
  1.5 1.7 copy-start
  3.2 0.8 copy-start.1

commit v2 on v1

v2 whole, which is shorter than its diff:
```python
import functools

import jax
import jax.numpy as jnp
from jax import lax
from jax.experimental import pallas as pl
from jax.experimental.pallas import tpu as pltpu
from jax.sharding import PartitionSpec as P

EDGE = 128
PANEL = 16
CHAINS = 1
LAG_ROW = 8
LAG_COL = 2
NEAR = 4
FAR_FIRST = True
MESH = pl.DeviceIdType.MESH
HIGH = lax.Precision.HIGHEST
F32 = jnp.float32
BF16 = jnp.bfloat16


def kernel(
    nr, nc, slots, order,
    tiles_hbm, start_hbm, table, cell,
    ritz_ref, gram_ref,
    tiles, start, dense, rbuf, cbuf, scale_r, scale_c,
    sT, w1, w2, w3, w4, x4,
    kept, given, land1, land2, gpart, ga, gs, gb, gfull, elim,
    load_sem, send_sem, recv_sem,
):
    me_of = {"row": lax.axis_index("row"), "col": lax.axis_index("col")}
    me_r, me_c = me_of["row"], me_of["col"]
    size = {"row": nr, "col": nc}
    deep = EDGE // CHAINS
    pending = []

    def lanes(tile):
        return pl.ds(pl.multiple_of(tile * EDGE, EDGE), EDGE)

    def copy(x, axis, peer, src, dst, slot):
        return pltpu.make_async_remote_copy(
            src_ref=src, dst_ref=dst, send_sem=send_sem.at[x], recv_sem=recv_sem.at[x, slot],
            device_id={axis: peer}, device_id_type=MESH,
        )

    def arrived(x, axis, ref, slot):
        copy(x, axis, me_of[axis], ref, ref, slot).wait_recv()

    def sent(x, axis, ref):
        pending.append(lambda: copy(x, axis, me_of[axis], ref, ref, 0).wait_send())

    def flush():
        while pending:
            pending.pop(0)()

    def place(axis):
        me = me_of[axis]
        return size[axis] // 2, me // 2, lax.rem(me, 2), me + 1 - 2 * lax.rem(me, 2)

    def group_at(axis, k):
        groups, mine, _, _ = place(axis)
        return lax.rem(mine + groups // 2 + (k + 1) // 2 * (2 * lax.rem(k, 2) - 1) + groups, groups)

    def others(axis, body):
        @pl.loop(0, size[axis])
        def _(k):
            peer = group_at(axis, k // 2) * 2 + lax.rem(k, 2)

            @pl.when(peer != me_of[axis])
            def _():
                body(peer)

    def send_all(x, axis, src_of, dst):
        others(axis, lambda peer: copy(x, axis, peer, src_of(peer), dst, me_of[axis]).start())

    def wait_all(x, axis, dst_of):
        n, me = size[axis], me_of[axis]

        @pl.loop(1, n)
        def _(k):
            source = lax.rem(me + k, n)
            arrived(x, axis, dst_of(source), source)

    load = pltpu.make_async_copy(tiles_hbm, tiles.at[pl.ds(0, slots)], load_sem.at[0])
    load.start()
    load_start = pltpu.make_async_copy(start_hbm, start, load_sem.at[1])
    load_start.start()
    barrier = pltpu.get_barrier_semaphore()
    for axis in ("row", "col"):
        others(axis, lambda peer, axis=axis: pl.semaphore_signal(
            barrier, inc=1, device_id={axis: peer}, device_id_type=MESH
        ))

    def depth(s):
        return pl.ds(s * deep, deep)

    whole = pl.ds(0, EDGE)

    def gather_send(x, axis, rows, tile, w):
        groups, mine, side, partner = place(axis)
        here = w.at[rows, lanes(me_of[axis])]
        w[rows, lanes(me_of[axis])] = tile

        @pl.loop(0, groups - 1)
        def _(k):
            copy(x, axis, group_at(axis, order_of(k, groups)) * 2 + side, here, here, mine).start()

        copy(x, axis, partner, here, here, groups + mine).start()
        sent(x, axis, w.at[rows, pl.ds(0, groups * EDGE)])

    def gather_pass(x, axis, rows, w, begin=0, end=None):
        groups, mine, side, partner = place(axis)
        last = end is None

        @pl.loop(begin, groups - 1 if last else end)
        def _(k):
            g = group_at(axis, order_of(k, groups))
            here = w.at[rows, lanes(g * 2 + side)]
            arrived(x, axis, here, g)
            copy(x + 1, axis, partner, here, here, groups + g).start()

        if last:
            sent(x + 1, axis, w.at[rows, pl.ds(0, (groups - 1) * EDGE)])

    def order_of(k, groups):
        return k if FAR_FIRST else groups - 2 - k

    def gather_wait(x, axis, rows, w):
        groups, mine, side, partner = place(axis)
        arrived(x, axis, w.at[rows, lanes(partner)], groups + mine)

        @pl.loop(0, groups - 1)
        def _(k):
            g = group_at(axis, order_of(k, groups))
            arrived(x + 1, axis, w.at[rows, lanes(g * 2 + 1 - side)], groups + g)

    def product(x, axis, rows, which, w, lag, between=None):
        groups, mine, side, partner = place(axis)
        keep, give, land = kept.at[which], given.at[which], land1.at[which]

        def multiply(k):
            g = group_at(axis, k)
            wide = pl.ds(pl.multiple_of(g * 2 * EDGE, 2 * EDGE), 2 * EDGE)
            if axis == "row":
                y = jnp.dot(w[rows, :], dense[:, wide], preferred_element_type=F32)
            else:
                y = lax.dot_general(
                    w[rows, :], dense[wide, :], (((1,), (1,)), ((), ())),
                    preferred_element_type=F32,
                )
            first, second = y[:, :EDGE], y[:, EDGE:]
            keep[g, rows, :] = jnp.where(side == 0, first, second)
            give[g, rows, :] = jnp.where(side == 0, second, first)
            copy(x, axis, partner, give.at[g, rows, :], land.at[g, rows, :], g).start()

        lag = lag * groups // 8

        @pl.loop(0, groups)
        def _(k):
            multiply(k)
            if lag < groups:
                @pl.when(k >= lag)
                def _():
                    pair_sum(x, axis, rows, which, k - lag)

        if between:
            between()

        @pl.loop(groups - lag, groups)
        def _(k):
            pair_sum(x, axis, rows, which, k)

        sent(x, axis, give.at[:, rows, :])
        sent(x + 1, axis, keep.at[pl.ds(0, groups - 1), rows, :])

    def pair_sum(x, axis, rows, which, k):
        groups, mine, side, partner = place(axis)
        keep, land = kept.at[which], land1.at[which]
        g = group_at(axis, k)
        arrived(x, axis, land.at[g, rows, :], g)
        keep[g, rows, :] = keep[g, rows, :] + land[g, rows, :]

        @pl.when(k < groups - 1)
        def _():
            copy(
                x + 1, axis, g * 2 + side, keep.at[g, rows, :], land2.at[which, mine, rows, :], mine
            ).start()

    def total_sum(x, axis, rows, which):
        groups, mine, side, partner = place(axis)
        land = land2.at[which]

        def add(k, total):
            g = group_at(axis, groups - 2 - k)
            arrived(x + 1, axis, land.at[g, rows, :], g)
            return total + land[g, rows, :]

        return lax.fori_loop(0, groups - 1, add, kept[which, mine, rows, :])

    chains = [depth(s) for s in range(CHAINS)]
    lag = {"row": LAG_ROW, "col": LAG_COL}

    tiles[slots] = jnp.zeros((EDGE, EDGE), BF16)
    load_start.wait()
    sT[:, lanes(me_c)] = start[...].astype(F32).T.astype(BF16)
    load.wait()

    def fold(s, total):
        return total + jnp.where(cell[s] == 0, tiles[s], jnp.zeros((EDGE, EDGE), BF16))

    tiles[slots + 1] = lax.fori_loop(0, slots, fold, jnp.zeros((EDGE, EDGE), BF16))

    @pl.loop(0, nc)
    def _(i):
        most = jnp.zeros((EDGE, EDGE), BF16)
        for j in range(nr):
            which = table[i * nr + j]
            if j == 0:
                which = jnp.where(i == 0, slots + 1, which)
            tile = tiles[which]
            dense[lanes(i), j * EDGE:(j + 1) * EDGE] = tile
            most = jnp.maximum(most, jnp.abs(tile))
        rbuf[me_c, pl.ds(i, 1), :] = jnp.max(most.astype(F32).T, axis=0, keepdims=True)

    pl.semaphore_wait(barrier, nr + nc - 2)
    gather_send(0, "col", whole, sT[:, lanes(me_c)], sT)
    send_all(2, "col", lambda peer: rbuf.at[me_c], rbuf.at[me_c])
    sent(2, "col", rbuf.at[pl.ds(0, nc - 1)])

    @pl.loop(0, nr)
    def _(j):
        most = jnp.zeros((EDGE, EDGE), BF16)
        for i in range(nc):
            most = jnp.maximum(most, jnp.abs(dense[i * EDGE:(i + 1) * EDGE, lanes(j)]))
        cbuf[me_r, pl.ds(j, 1), :] = jnp.max(most.astype(F32), axis=0, keepdims=True)

    gather_pass(0, "col", whole, sT)
    wait_all(2, "col", lambda source: rbuf.at[source])
    scale_r[...] = 1.0 / jnp.sqrt(jnp.max(rbuf[...], axis=0))
    mine_r = scale_r[pl.ds(me_c, 1), :]
    gather_wait(0, "col", whole, sT)
    for t in range(nc):
        here = slice(t * EDGE, (t + 1) * EDGE)
        w1[:, here] = (scale_r[t:t + 1, :] * sT[:, here].astype(F32)).astype(BF16)
    x = 4

    def after_product():
        send_all(3, "row", lambda peer: cbuf.at[me_r], cbuf.at[me_r])
        sent(3, "row", cbuf.at[pl.ds(0, nr - 1)])

    for s, rows in enumerate(chains):
        product(x + 2 * s, "row", rows, 0, w1, lag["row"], after_product if s == 0 else None)
    flush()
    wait_all(3, "row", lambda source: cbuf.at[source])
    scale_c[...] = 1.0 / jnp.sqrt(jnp.max(cbuf[...], axis=0))
    mine_c = scale_c[pl.ds(me_r, 1), :]

    def turn(x, axis, which, scale, w, other):
        y = x + 2 * CHAINS
        for s, rows in enumerate(chains):
            tile = (scale * scale * total_sum(x + 2 * s, axis, rows, which)).astype(BF16)
            gather_send(y + 2 * s, axis, rows, tile, w)
        for s, rows in enumerate(chains):
            gather_pass(y + 2 * s, axis, rows, w)
        z = y + 2 * CHAINS
        for s, rows in enumerate(chains):
            gather_wait(y + 2 * s, axis, rows, w)
            product(z + 2 * s, other, rows, which + 1, w, lag[other])
        flush()
        return z

    x = turn(x, "row", 0, mine_c, w2, "col")
    x = turn(x, "col", 1, mine_r, w3, "row")
    iterate = mine_c * jnp.concatenate(
        [total_sum(x + 2 * s, "row", rows, 2) for s, rows in enumerate(chains)], axis=0
    )
    x += 2 * CHAINS

    def outer(v):
        return lax.dot_general(
            v, v, (((1,), (1,)), ((), ())), precision=HIGH, preferred_element_type=F32
        )

    share = EDGE // nc

    def strip(p):
        return pl.ds(pl.multiple_of(p * share, share), share)

    def gram_sum(x, which, local, first=None, second=None, third=None):
        part, a, s, b, full = gpart.at[which], ga.at[which], gs.at[which], gb.at[which], gfull.at[which]
        part[...] = local
        send_all(x, "col", lambda peer: part.at[strip(peer)], a.at[me_c])
        sent(x, "col", a.at[pl.ds(0, nc - 1)])
        a[me_c] = part[strip(me_c), :]
        if first:
            first()
        wait_all(x, "col", lambda source: a.at[source])
        mine = jnp.sum(a[...], axis=0)
        s[...] = mine
        send_all(x + 1, "row", lambda peer: s, b.at[me_r])
        sent(x + 1, "row", b.at[pl.ds(0, nr - 1)])
        b[me_r] = mine
        if second:
            second()
        wait_all(x + 1, "row", lambda source: b.at[source])
        full[strip(me_c), :] = jnp.sum(b[...], axis=0) / order
        send_all(x + 2, "col", lambda peer: full.at[strip(me_c)], full.at[strip(me_c)])
        sent(x + 2, "col", a.at[pl.ds(0, nc - 1)])
        if third:
            third()
        wait_all(x + 2, "col", lambda source: full.at[strip(source)])
        return full[...]

    near = NEAR * nr // 16
    gram = gram_sum(
        x, 0, outer(iterate),
        lambda: gather_send(x + 3, "row", whole, iterate, x4),
        lambda: gather_pass(x + 3, "row", whole, x4, 0, near),
        lambda: gather_pass(x + 3, "row", whole, x4, near),
    )
    flush()

    elim[:, :EDGE] = gram
    row_id = lax.broadcasted_iota(jnp.int32, (EDGE, EDGE), 0)
    lane_id = lax.broadcasted_iota(jnp.int32, (EDGE, EDGE), 1)
    elim[:, EDGE:] = jnp.where(row_id == lane_id, 1.0, 0.0)
    lane = lax.broadcasted_iota(jnp.int32, (PANEL, EDGE), 1)
    sub = lax.broadcasted_iota(jnp.int32, (PANEL, EDGE), 0)

    @pl.loop(0, EDGE // PANEL)
    def _(p):
        rows = pl.ds(pl.multiple_of(p * PANEL, PANEL), PANEL)
        left = elim[rows, :EDGE]
        right = elim[rows, EDGE:]
        column = [
            jnp.broadcast_to(
                jnp.sum(jnp.where(lane == p * PANEL + k, left, 0.0), axis=1, keepdims=True),
                (PANEL, EDGE),
            )
            for k in range(PANEL)
        ]
        for k in range(PANEL):
            inv = 1.0 / jnp.sqrt(column[k][k:k + 1, :])
            step = jnp.where(sub > k, column[k] * inv, 0.0)
            l_row = left[k:k + 1, :] * inv
            r_row = right[k:k + 1, :] * inv
            left = jnp.where(sub == k, l_row, left - step * l_row)
            right = jnp.where(sub == k, r_row, right - step * r_row)
            for m in range(k + 1, PANEL):
                column[m] = column[m] - step * (column[m][k:k + 1, :] * inv)
        elim[rows, :EDGE] = left
        elim[rows, EDGE:] = right
        later = jnp.where(lane >= (p + 1) * PANEL, left, 0.0)
        both = jnp.concatenate([left, right], axis=1)
        elim[...] -= lax.dot_general(
            later, both, (((0,), (0,)), ((), ())), precision=HIGH, preferred_element_type=F32
        )

    gather_wait(x + 3, "row", whole, x4)
    inverse = elim[:, EDGE:]
    for t in range(0, nr, 2):
        here = slice(t * EDGE, (t + 2) * EDGE)
        basis = jnp.dot(inverse, x4[:, here], precision=HIGH, preferred_element_type=F32)
        both = jnp.concatenate([scale_c[t:t + 1, :], scale_c[t + 1:t + 2, :]], axis=1)
        w4[:, here] = (both * basis).astype(BF16)
    x += 5
    product(x, "col", whole, 3, w4, lag["col"])
    ritz = mine_r * total_sum(x, "col", whole, 3)
    x += 2
    ritz_ref[...] = ritz.T
    gram_ref[...] = gram_sum(x, 1, outer(ritz), flush)
    flush()


def local(affinity_tiles, tile_index, start_block):
    nr, nc = lax.axis_size("row"), lax.axis_size("col")
    stored = affinity_tiles[0, 0]
    index = tile_index[0, 0]
    slots = stored.shape[0]
    cell = index[0] * nr + index[1]
    hit = cell[:, None] == jnp.arange(nr * nc, dtype=jnp.int32)[None, :]
    number = jnp.arange(slots, dtype=jnp.int32)[:, None]
    table = jnp.min(jnp.where(hit, number, slots), axis=0)
    most = max(nr, nc)
    groups = most // 2
    share = EDGE // nc
    tile = (EDGE, EDGE)
    exchanges = 14 + 10 * CHAINS
    vmem = pltpu.VMEM
    return pl.pallas_call(
        functools.partial(kernel, nr, nc, slots, nr * nc * EDGE),
        out_shape=(jax.ShapeDtypeStruct(tile, F32), jax.ShapeDtypeStruct(tile, F32)),
        in_specs=[
            pl.BlockSpec(memory_space=pl.ANY),
            pl.BlockSpec(memory_space=pl.ANY),
            pl.BlockSpec(memory_space=pltpu.SMEM),
            pl.BlockSpec(memory_space=pltpu.SMEM),
        ],
        out_specs=(pl.BlockSpec(memory_space=pltpu.VMEM), pl.BlockSpec(memory_space=pltpu.VMEM)),
        scratch_shapes=[
            vmem((slots + 2, *tile), BF16),
            vmem(tile, BF16),
            vmem((nc * EDGE, nr * EDGE), BF16),
            vmem((nc, nc, EDGE), F32),
            vmem((nr, nr, EDGE), F32),
            vmem((nc, EDGE), F32),
            vmem((nr, EDGE), F32),
            vmem((EDGE, nc * EDGE), BF16),
            vmem((EDGE, nc * EDGE), BF16),
            vmem((EDGE, nr * EDGE), BF16),
            vmem((EDGE, nc * EDGE), BF16),
            vmem((EDGE, nr * EDGE), BF16),
            vmem((EDGE, nr * EDGE), F32),
            vmem((4, groups, *tile), F32),
            vmem((4, groups, *tile), F32),
            vmem((4, groups, *tile), F32),
            vmem((4, groups, *tile), F32),
            vmem((2, *tile), F32),
            vmem((2, nc, share, EDGE), F32),
            vmem((2, share, EDGE), F32),
            vmem((2, nr, share, EDGE), F32),
            vmem((2, *tile), F32),
            vmem((EDGE, 2 * EDGE), F32),
            pltpu.SemaphoreType.DMA((2,)),
            pltpu.SemaphoreType.DMA((exchanges,)),
            pltpu.SemaphoreType.DMA((exchanges, most)),
        ],
        compiler_params=pltpu.CompilerParams(
            collective_id=0, has_side_effects=True, vmem_limit_bytes=48 * 2**20
        ),
    )(stored, start_block, table, cell)


def solution(mesh):
    placed = (
        P("row", "col", None, None, None),
        P("row", "col", None, None),
        P(("row", "col"), None),
    )
    return jax.shard_map(
        local, mesh=mesh, in_specs=placed, out_specs=(P(("row", "col"), None), P()), check_vma=False
    )
```

time: 194 us -> 153 us (0.79)
  Pallas kernels: 188 us -> 147 us
    pallas_call x1, Pallas kernels: 188 us -> 147 us  [local(): pl.pallas_call(functools.partial(kernel, nr, nc, slots, nr * nc * EDGE),...]
where the time goes in v2:
time: 153 us
  Pallas kernels  147 us (96%)
  local copies, waits for them, and re-layouts  3.75 us (2%)
    pallas_call x1, Pallas kernels, local(): pl.pallas_call(functools.partial(kernel, nr, nc, slots, nr * nc * EDGE),...  147 us
    unnamed x6, local copies, waits for them, and re-layouts  3.75 us

profile of v2, /device:TPU:1, one launch (start us, length us, event | category | flops | bytes accessed | tf_op | source)
XLA Modules:
  0.0 152.7 jit_solution(4011985729064606582)
XLA Ops:
  0.6 0.8 add_bitcast_fusion.cell
  1.4 0.1 select_reduce_fusion.table
  1.5 0.0 copy-start
  1.5 1.7 %copy-done = bf16[1,1,80,128,128]{4,3,2,1,0:T(8,128)(2,1)S(1)} copy-done((bf16[1,1,80,128,128]{4,3,2,1,0:T(8,128)(2,1)S(1)}, bf16[1,1,80,128,128]{4,3,2,1,0:T(8,128)(2,1)}, u32[]{:S(2)}) %copy-start) | copy-done | bytes 2621464
  3.2 0.0 copy-start.1
  3.2 0.8 copy-done.1
  4.0 147.4 %shard_map.50 = (f32[128,128]{1,0:T(8,128)S(1)}, f32[128,128]{1,0:T(8,128)S(1)}) custom-call(bf16[80,128,128]{2,1,0:T(8,128)(2,1)S(1)} %bitcast.3, bf16[128,128]{1,0:T(8,128)(2,1)S(1)} %copy-done.1, s32[256]{0:T(256)S(1)} %select_reduce_fusion.table, s32[80]{0:T(128)S(1)} %add_bitcast_fusion.cell), custom_call_target="tpu_custom_call" | custom-call | tf_op jit(solution)/shard_map/pallas_call | solution.py:391
  151.4 0.6 copy.7
  152.0 0.6 copy.8
Async XLA Ops:
  1.5 1.7 %copy-start = (bf16[1,1,80,128,128]{4,3,2,1,0:T(8,128)(2,1)S(1)}, bf16[1,1,80,128,128]{4,3,2,1,0:T(8,128)(2,1)}, u32[]{:S(2)}) copy-start(bf16[1,1,80,128,128]{4,3,2,1,0:T(8,128)(2,1)} %param.3) | copy-start | bytes 7864324
  3.2 0.8 copy-start.1

commit v3 on v2

--- a/solution.py
+++ b/solution.py
@@ -209,7 +209,7 @@
     def fold(s, total):
         return total + jnp.where(cell[s] == 0, tiles[s], jnp.zeros((EDGE, EDGE), BF16))
 
-    tiles[slots + 1] = lax.fori_loop(0, slots, fold, jnp.zeros((EDGE, EDGE), BF16))
+    tiles[slots + 1] = lax.fori_loop(0, slots, fold, jnp.zeros((EDGE, EDGE), BF16), unroll=8)
 
     @pl.loop(0, nc)
     def _(i):
@@ -219,7 +219,6 @@
             if j == 0:
                 which = jnp.where(i == 0, slots + 1, which)
             tile = tiles[which]
-            dense[lanes(i), j * EDGE:(j + 1) * EDGE] = tile
             most = jnp.maximum(most, jnp.abs(tile))
         rbuf[me_c, pl.ds(i, 1), :] = jnp.max(most.astype(F32).T, axis=0, keepdims=True)
 
@@ -232,9 +231,16 @@
     def _(j):
         most = jnp.zeros((EDGE, EDGE), BF16)
         for i in range(nc):
-            most = jnp.maximum(most, jnp.abs(dense[i * EDGE:(i + 1) * EDGE, lanes(j)]))
+            which = table[i * nr + j]
+            if i == 0:
+                which = jnp.where(j == 0, slots + 1, which)
+            tile = tiles[which]
+            dense[i * EDGE:(i + 1) * EDGE, lanes(j)] = tile
+            most = jnp.maximum(most, jnp.abs(tile))
         cbuf[me_r, pl.ds(j, 1), :] = jnp.max(most.astype(F32), axis=0, keepdims=True)
 
+    send_all(3, "row", lambda peer: cbuf.at[me_r], cbuf.at[me_r])
+    sent(3, "row", cbuf.at[pl.ds(0, nr - 1)])
     gather_pass(0, "col", whole, sT)
     wait_all(2, "col", lambda source: rbuf.at[source])
     scale_r[...] = 1.0 / jnp.sqrt(jnp.max(rbuf[...], axis=0))
@@ -245,12 +251,8 @@
         w1[:, here] = (scale_r[t:t + 1, :] * sT[:, here].astype(F32)).astype(BF16)
     x = 4
 
-    def after_product():
-        send_all(3, "row", lambda peer: cbuf.at[me_r], cbuf.at[me_r])
-        sent(3, "row", cbuf.at[pl.ds(0, nr - 1)])
-
     for s, rows in enumerate(chains):
-        product(x + 2 * s, "row", rows, 0, w1, lag["row"], after_product if s == 0 else None)
+        product(x + 2 * s, "row", rows, 0, w1, lag["row"])
     flush()
     wait_all(3, "row", lambda source: cbuf.at[source])
     scale_c[...] = 1.0 / jnp.sqrt(jnp.max(cbuf[...], axis=0))

time: 153 us -> 150 us (0.980)
  Pallas kernels: 147 us -> 145 us
    pallas_call x1, Pallas kernels: 147 us -> 145 us  [local(): pl.pallas_call(functools.partial(kernel, nr, nc, slots, nr * nc * EDGE),...]
where the time goes in v3:
time: 150 us
  Pallas kernels  145 us (97%)
  local copies, waits for them, and re-layouts  3.75 us (2%)
    pallas_call x1, Pallas kernels, local(): pl.pallas_call(functools.partial(kernel, nr, nc, slots, nr * nc * EDGE),...  145 us
    unnamed x6, local copies, waits for them, and re-layouts  3.75 us

profile of v3, /device:TPU:1, one launch (start us, length us, event | category | flops | bytes accessed | tf_op | source)
XLA Modules:
  0.0 150.2 jit_solution(1469983903104899102)
XLA Ops:
  0.6 0.8 add_bitcast_fusion.cell
  1.4 0.1 select_reduce_fusion.table
  1.5 0.0 copy-start
  1.5 1.7 %copy-done = bf16[1,1,80,128,128]{4,3,2,1,0:T(8,128)(2,1)S(1)} copy-done((bf16[1,1,80,128,128]{4,3,2,1,0:T(8,128)(2,1)S(1)}, bf16[1,1,80,128,128]{4,3,2,1,0:T(8,128)(2,1)}, u32[]{:S(2)}) %copy-start) | copy-done | bytes 2621464
  3.2 0.0 copy-start.1
  3.2 0.8 copy-done.1
  4.0 144.9 %shard_map.50 = (f32[128,128]{1,0:T(8,128)S(1)}, f32[128,128]{1,0:T(8,128)S(1)}) custom-call(bf16[80,128,128]{2,1,0:T(8,128)(2,1)S(1)} %bitcast.3, bf16[128,128]{1,0:T(8,128)(2,1)S(1)} %copy-done.1, s32[256]{0:T(256)S(1)} %select_reduce_fusion.table, s32[80]{0:T(128)S(1)} %add_bitcast_fusion.cell), custom_call_target="tpu_custom_call" | custom-call | tf_op jit(solution)/shard_map/pallas_call | solution.py:393
  148.9 0.6 copy.7
  149.6 0.6 copy.8
Async XLA Ops:
  1.5 1.7 %copy-start = (bf16[1,1,80,128,128]{4,3,2,1,0:T(8,128)(2,1)S(1)}, bf16[1,1,80,128,128]{4,3,2,1,0:T(8,128)(2,1)}, u32[]{:S(2)}) copy-start(bf16[1,1,80,128,128]{4,3,2,1,0:T(8,128)(2,1)} %param.3) | copy-start | bytes 7864324
  3.2 0.8 copy-start.1

commit v4 on v3

--- a/solution.py
+++ b/solution.py
@@ -9,9 +9,8 @@
 
 EDGE = 128
 PANEL = 16
-CHAINS = 1
-LAG_ROW = 8
-LAG_COL = 2
+CHAINS = 2
+LAG = {"row": 8, "col": 2}
 NEAR = 4
 FAR_FIRST = True
 MESH = pl.DeviceIdType.MESH
@@ -96,6 +95,7 @@
         return pl.ds(s * deep, deep)
 
     whole = pl.ds(0, EDGE)
+    chains = [depth(s) for s in range(CHAINS)]
 
     def gather_send(x, axis, rows, tile, w):
         groups, mine, side, partner = place(axis)
@@ -135,44 +135,78 @@
             g = group_at(axis, order_of(k, groups))
             arrived(x + 1, axis, w.at[rows, lanes(g * 2 + 1 - side)], groups + g)
 
-    def product(x, axis, rows, which, w, lag, between=None):
-        groups, mine, side, partner = place(axis)
-        keep, give, land = kept.at[which], given.at[which], land1.at[which]
-
-        def multiply(k):
-            g = group_at(axis, k)
-            wide = pl.ds(pl.multiple_of(g * 2 * EDGE, 2 * EDGE), 2 * EDGE)
-            if axis == "row":
-                y = jnp.dot(w[rows, :], dense[:, wide], preferred_element_type=F32)
-            else:
-                y = lax.dot_general(
-                    w[rows, :], dense[wide, :], (((1,), (1,)), ((), ())),
-                    preferred_element_type=F32,
-                )
-            first, second = y[:, :EDGE], y[:, EDGE:]
-            keep[g, rows, :] = jnp.where(side == 0, first, second)
-            give[g, rows, :] = jnp.where(side == 0, second, first)
-            copy(x, axis, partner, give.at[g, rows, :], land.at[g, rows, :], g).start()
-
-        lag = lag * groups // 8
+    def give_one(x, axis, rows, which, k):
+        groups, mine, side, partner = place(axis)
+        g = group_at(axis, k)
+        copy(
+            x, axis, partner, given.at[which, g, rows, :], land1.at[which, g, rows, :], g
+        ).start()
+
+    def multiply(axis, rows, which, w, k):
+        groups, mine, side, partner = place(axis)
+        g = group_at(axis, k)
+        wide = pl.ds(pl.multiple_of(g * 2 * EDGE, 2 * EDGE), 2 * EDGE)
+        if axis == "row":
+            y = jnp.dot(w[rows, :], dense[:, wide], preferred_element_type=F32)
+        else:
+            y = lax.dot_general(
+                w[rows, :], dense[wide, :], (((1,), (1,)), ((), ())),
+                preferred_element_type=F32,
+            )
+        first, second = y[:, :EDGE], y[:, EDGE:]
+        kept[which, g, rows, :] = jnp.where(side == 0, first, second)
+        given[which, g, rows, :] = jnp.where(side == 0, second, first)
+
+    def products(x, axis, which, w, ready):
+        groups = size[axis] // 2
+        lag = min(LAG[axis], groups)
+        for s, rows in enumerate(chains):
+            ready(s, rows)
+
+            @pl.loop(0, groups)
+            def _(k, s=s, rows=rows):
+                multiply(axis, rows, which, w, k)
+                give_one(x + 2 * s, axis, rows, which, k)
+                if lag < groups:
+                    @pl.when(k >= lag)
+                    def _():
+                        pair_sum(x + 2 * s, axis, rows, which, k - lag)
+
+            if lag < groups:
+                pair_sums(x + 2 * s, axis, rows, which, groups - lag)
+        if lag == groups:
+            for s, rows in enumerate(chains):
+                pair_sums(x + 2 * s, axis, rows, which, 0)
+        products_sent(x, axis, which)
+
+    def joint_product(x, axis, which, w):
+        groups = size[axis] // 2
 
         @pl.loop(0, groups)
         def _(k):
-            multiply(k)
-            if lag < groups:
-                @pl.when(k >= lag)
-                def _():
-                    pair_sum(x, axis, rows, which, k - lag)
-
-        if between:
-            between()
-
-        @pl.loop(groups - lag, groups)
+            multiply(axis, whole, which, w, k)
+            give_one(x, axis, chains[0], which, k)
+
+        for s, rows in enumerate(chains):
+            if s:
+                @pl.loop(0, groups)
+                def _(k, s=s, rows=rows):
+                    give_one(x + 2 * s, axis, rows, which, k)
+
+        for s, rows in enumerate(chains):
+            pair_sums(x + 2 * s, axis, rows, which, 0)
+        products_sent(x, axis, which)
+
+    def products_sent(x, axis, which):
+        groups = size[axis] // 2
+        for s, rows in enumerate(chains):
+            sent(x + 2 * s, axis, given.at[which, :, rows, :])
+            sent(x + 2 * s + 1, axis, kept.at[which, pl.ds(0, groups - 1), rows, :])
+
+    def pair_sums(x, axis, rows, which, begin):
+        @pl.loop(begin, size[axis] // 2)
         def _(k):
             pair_sum(x, axis, rows, which, k)
-
-        sent(x, axis, give.at[:, rows, :])
-        sent(x + 1, axis, keep.at[pl.ds(0, groups - 1), rows, :])
 
     def pair_sum(x, axis, rows, which, k):
         groups, mine, side, partner = place(axis)
@@ -197,9 +231,6 @@
             return total + land[g, rows, :]
 
         return lax.fori_loop(0, groups - 1, add, kept[which, mine, rows, :])
-
-    chains = [depth(s) for s in range(CHAINS)]
-    lag = {"row": LAG_ROW, "col": LAG_COL}
 
     tiles[slots] = jnp.zeros((EDGE, EDGE), BF16)
     load_start.wait()
@@ -251,8 +282,7 @@
         w1[:, here] = (scale_r[t:t + 1, :] * sT[:, here].astype(F32)).astype(BF16)
     x = 4
 
-    for s, rows in enumerate(chains):
-        product(x + 2 * s, "row", rows, 0, w1, lag["row"])
+    joint_product(x, "row", 0, w1)
     flush()
     wait_all(3, "row", lambda source: cbuf.at[source])
     scale_c[...] = 1.0 / jnp.sqrt(jnp.max(cbuf[...], axis=0))
@@ -266,9 +296,9 @@
         for s, rows in enumerate(chains):
             gather_pass(y + 2 * s, axis, rows, w)
         z = y + 2 * CHAINS
-        for s, rows in enumerate(chains):
-            gather_wait(y + 2 * s, axis, rows, w)
-            product(z + 2 * s, other, rows, which + 1, w, lag[other])
+        products(
+            z, other, which + 1, w, lambda s, rows: gather_wait(y + 2 * s, axis, rows, w)
+        )
         flush()
         return z
 
@@ -367,7 +397,8 @@
         both = jnp.concatenate([scale_c[t:t + 1, :], scale_c[t + 1:t + 2, :]], axis=1)
         w4[:, here] = (both * basis).astype(BF16)
     x += 5
-    product(x, "col", whole, 3, w4, lag["col"])
+    chains = [whole]
+    products(x, "col", 3, w4, lambda s, rows: None)
     ritz = mine_r * total_sum(x, "col", whole, 3)
     x += 2
     ritz_ref[...] = ritz.T

time: 150 us -> 148 us (0.987)
  Pallas kernels: 145 us -> 143 us
    pallas_call x1, Pallas kernels: 145 us -> 143 us  [local(): pl.pallas_call(functools.partial(kernel, nr, nc, slots, nr * nc * EDGE),...]
where the time goes in v4:
time: 148 us
  Pallas kernels  143 us (97%)
  local copies, waits for them, and re-layouts  3.75 us (3%)
    pallas_call x1, Pallas kernels, local(): pl.pallas_call(functools.partial(kernel, nr, nc, slots, nr * nc * EDGE),...  143 us
    unnamed x6, local copies, waits for them, and re-layouts  3.75 us

profile of v4, /device:TPU:1, one launch (start us, length us, event | category | flops | bytes accessed | tf_op | source)
XLA Modules:
  0.0 147.9 jit_solution(8802595096567062740)
XLA Ops:
  0.6 0.8 add_bitcast_fusion.cell
  1.4 0.1 select_reduce_fusion.table
  1.5 0.0 copy-start
  1.5 1.7 %copy-done = bf16[1,1,80,128,128]{4,3,2,1,0:T(8,128)(2,1)S(1)} copy-done((bf16[1,1,80,128,128]{4,3,2,1,0:T(8,128)(2,1)S(1)}, bf16[1,1,80,128,128]{4,3,2,1,0:T(8,128)(2,1)}, u32[]{:S(2)}) %copy-start) | copy-done | bytes 2621464
  3.2 0.0 copy-start.1
  3.2 0.8 copy-done.1
  4.0 142.7 %shard_map.50 = (f32[128,128]{1,0:T(8,128)S(1)}, f32[128,128]{1,0:T(8,128)S(1)}) custom-call(bf16[80,128,128]{2,1,0:T(8,128)(2,1)S(1)} %bitcast.3, bf16[128,128]{1,0:T(8,128)(2,1)S(1)} %copy-done.1, s32[256]{0:T(256)S(1)} %select_reduce_fusion.table, s32[80]{0:T(128)S(1)} %add_bitcast_fusion.cell), custom_call_target="tpu_custom_call" | custom-call | tf_op jit(solution)/shard_map/pallas_call | solution.py:424
  146.7 0.6 copy.7
  147.3 0.6 copy.8
Async XLA Ops:
  1.5 1.7 %copy-start = (bf16[1,1,80,128,128]{4,3,2,1,0:T(8,128)(2,1)S(1)}, bf16[1,1,80,128,128]{4,3,2,1,0:T(8,128)(2,1)}, u32[]{:S(2)}) copy-start(bf16[1,1,80,128,128]{4,3,2,1,0:T(8,128)(2,1)} %param.3) | copy-start | bytes 7864324
  3.2 0.8 copy-start.1

commit v5 on v4

--- a/solution.py
+++ b/solution.py
@@ -10,7 +10,7 @@
 EDGE = 128
 PANEL = 16
 CHAINS = 2
-LAG = {"row": 8, "col": 2}
+LAG = {"row": 8, "col": 3}
 NEAR = 4
 FAR_FIRST = True
 MESH = pl.DeviceIdType.MESH

time: 148 us -> 147 us (level)
  Pallas kernels: 143 us -> 141 us
where the time goes in v5:
time: 147 us
  Pallas kernels  141 us (96%)
  local copies, waits for them, and re-layouts  3.75 us (3%)
    pallas_call x1, Pallas kernels, local(): pl.pallas_call(functools.partial(kernel, nr, nc, slots, nr * nc * EDGE),...  141 us
    unnamed x6, local copies, waits for them, and re-layouts  3.75 us

profile of v5, /device:TPU:1, one launch (start us, length us, event | category | flops | bytes accessed | tf_op | source)
XLA Modules:
  0.0 146.7 jit_solution(16984056703655066119)
XLA Ops:
  0.6 0.8 add_bitcast_fusion.cell
  1.4 0.1 select_reduce_fusion.table
  1.5 0.0 copy-start
  1.5 1.7 %copy-done = bf16[1,1,80,128,128]{4,3,2,1,0:T(8,128)(2,1)S(1)} copy-done((bf16[1,1,80,128,128]{4,3,2,1,0:T(8,128)(2,1)S(1)}, bf16[1,1,80,128,128]{4,3,2,1,0:T(8,128)(2,1)}, u32[]{:S(2)}) %copy-start) | copy-done | bytes 2621464
  3.2 0.0 copy-start.1
  3.2 0.8 copy-done.1
  4.0 141.4 %shard_map.50 = (f32[128,128]{1,0:T(8,128)S(1)}, f32[128,128]{1,0:T(8,128)S(1)}) custom-call(bf16[80,128,128]{2,1,0:T(8,128)(2,1)S(1)} %bitcast.3, bf16[128,128]{1,0:T(8,128)(2,1)S(1)} %copy-done.1, s32[256]{0:T(256)S(1)} %select_reduce_fusion.table, s32[80]{0:T(128)S(1)} %add_bitcast_fusion.cell), custom_call_target="tpu_custom_call" | custom-call | tf_op jit(solution)/shard_map/pallas_call | solution.py:424
  145.4 0.6 copy.7
  146.0 0.6 copy.8
Async XLA Ops:
  1.5 1.7 %copy-start = (bf16[1,1,80,128,128]{4,3,2,1,0:T(8,128)(2,1)S(1)}, bf16[1,1,80,128,128]{4,3,2,1,0:T(8,128)(2,1)}, u32[]{:S(2)}) copy-start(bf16[1,1,80,128,128]{4,3,2,1,0:T(8,128)(2,1)} %param.3) | copy-start | bytes 7864324
  3.2 0.8 copy-start.1

commit v6 on v5

--- a/solution.py
+++ b/solution.py
@@ -391,18 +391,22 @@
 
     gather_wait(x + 3, "row", whole, x4)
     inverse = elim[:, EDGE:]
-    for t in range(0, nr, 2):
-        here = slice(t * EDGE, (t + 2) * EDGE)
+    for t in range(0, nr, 4):
+        here = slice(t * EDGE, (t + 4) * EDGE)
         basis = jnp.dot(inverse, x4[:, here], precision=HIGH, preferred_element_type=F32)
-        both = jnp.concatenate([scale_c[t:t + 1, :], scale_c[t + 1:t + 2, :]], axis=1)
+        both = jnp.concatenate([scale_c[t + i:t + i + 1, :] for i in range(4)], axis=1)
         w4[:, here] = (both * basis).astype(BF16)
     x += 5
     chains = [whole]
     products(x, "col", 3, w4, lambda s, rows: None)
     ritz = mine_r * total_sum(x, "col", whole, 3)
     x += 2
-    ritz_ref[...] = ritz.T
-    gram_ref[...] = gram_sum(x, 1, outer(ritz), flush)
+
+    def finish():
+        ritz_ref[...] = ritz.T
+        flush()
+
+    gram_ref[...] = gram_sum(x, 1, outer(ritz), finish)
     flush()
 
 

time: 147 us -> 147 us (level)
  no operation moved by 1% of the time
where the time goes in v6:
time: 147 us
  Pallas kernels  141 us (96%)
  local copies, waits for them, and re-layouts  3.75 us (3%)
    pallas_call x1, Pallas kernels, local(): pl.pallas_call(functools.partial(kernel, nr, nc, slots, nr * nc * EDGE),...  141 us
    unnamed x6, local copies, waits for them, and re-layouts  3.75 us

profile of v6, /device:TPU:1, one launch (start us, length us, event | category | flops | bytes accessed | tf_op | source)
XLA Modules:
  0.0 146.7 jit_solution(7125754215917609306)
XLA Ops:
  0.6 0.8 add_bitcast_fusion.cell
  1.4 0.1 select_reduce_fusion.table
  1.5 0.0 copy-start
  1.5 1.7 %copy-done = bf16[1,1,80,128,128]{4,3,2,1,0:T(8,128)(2,1)S(1)} copy-done((bf16[1,1,80,128,128]{4,3,2,1,0:T(8,128)(2,1)S(1)}, bf16[1,1,80,128,128]{4,3,2,1,0:T(8,128)(2,1)}, u32[]{:S(2)}) %copy-start) | copy-done | bytes 2621464
  3.2 0.0 copy-start.1
  3.2 0.8 copy-done.1
  4.0 141.4 %shard_map.50 = (f32[128,128]{1,0:T(8,128)S(1)}, f32[128,128]{1,0:T(8,128)S(1)}) custom-call(bf16[80,128,128]{2,1,0:T(8,128)(2,1)S(1)} %bitcast.3, bf16[128,128]{1,0:T(8,128)(2,1)S(1)} %copy-done.1, s32[256]{0:T(256)S(1)} %select_reduce_fusion.table, s32[80]{0:T(128)S(1)} %add_bitcast_fusion.cell), custom_call_target="tpu_custom_call" | custom-call | tf_op jit(solution)/shard_map/pallas_call | solution.py:428
  145.4 0.6 copy.7
  146.1 0.6 copy.8
Async XLA Ops:
  1.5 1.7 %copy-start = (bf16[1,1,80,128,128]{4,3,2,1,0:T(8,128)(2,1)S(1)}, bf16[1,1,80,128,128]{4,3,2,1,0:T(8,128)(2,1)}, u32[]{:S(2)}) copy-start(bf16[1,1,80,128,128]{4,3,2,1,0:T(8,128)(2,1)} %param.3) | copy-start | bytes 7864324
  3.2 0.8 copy-start.1
